TPU v7x, 128 devices: a whole 4x4x4 slice. The times are simulated.
128 devices in a mesh: group: 8 (over x, core), local: 16 (over y, z).
Axes of the slice: x: 4, y: 4, z: 4, core: 2. Of those that a mesh axis runs over, the one named last changes fastest.
Arguments:
- tokens: bfloat16 [2048, 3584], P(('group', 'local')), may hold values from -6 to 6
- out_grad: bfloat16 [2048, 3584], P(('group', 'local')), may hold values from -6 to 6
- expert_ids: int32 [2048, 8], P(('group', 'local')), may hold values from 0 to 127, as said below
- probs: bfloat16 [2048, 8], P(('group', 'local')), may hold values from 0.049804688 to 0.3984375
- w_gate: bfloat16 [128, 3584, 1024], P(('group', 'local')), may hold values from -0.09375 to 0.09375
- w_up: bfloat16 [128, 3584, 1024], P(('group', 'local')), may hold values from -0.09375 to 0.09375
- w_down: bfloat16 [128, 1024, 3584], P(('group', 'local')), may hold values from -0.1875 to 0.1875
Outputs:
- d_tokens: bfloat16 [2048, 3584], P(('group', 'local'))
Inputs may be any that keep to these rules, and one draw needn't show every extreme that they name: `expert_ids`: each token names 8 different experts, 2 in each of 4 node groups, expert e lying in node group e // 16. One node group, drawn from the seed, is chosen by every token. Within the tokens of one device the experts of one node group are named equally often, up to one, so that no expert is named more than 2 times by the tokens of one device; the experts of the common node group reach 2 on every device.
All inputs are finite; a program needn't handle non-finite values.
Results may differ from a plain program's by a relative error of at most 0.012.
Values may be sent and summed in bfloat16 or wider, within the bound.
A program may use at most 128 MiB of HBM per device.

v0:
```python
import jax
import jax.numpy as jnp
from jax import lax
from jax.sharding import PartitionSpec as P

TOP = 8
GROUPS_TOKEN = 4


def expert_backward(rows_in, rows_grad, rows_prob, w_gate, w_up, w_down):
    gate = jnp.dot(rows_in, w_gate, preferred_element_type=jnp.float32)
    upward = jnp.dot(rows_in, w_up, preferred_element_type=jnp.float32)
    contract = (((1,), (1,)), ((), ()))
    d_hidden = lax.dot_general(rows_grad, w_down, contract, preferred_element_type=jnp.float32)
    sigmoid = jax.nn.sigmoid(gate)
    d_gate = (d_hidden * upward * (sigmoid * (1.0 + gate * (1.0 - sigmoid)))).astype(jnp.bfloat16)
    d_up = (d_hidden * (gate * sigmoid)).astype(jnp.bfloat16)
    back = lax.dot_general(d_gate, w_gate, contract, preferred_element_type=jnp.float32)
    back = back + lax.dot_general(d_up, w_up, contract, preferred_element_type=jnp.float32)
    return (rows_prob.astype(jnp.float32)[:, None] * back).astype(jnp.bfloat16)


def ranks_within(targets, owners):
    onehot = (targets[:, None] == jnp.arange(owners, dtype=jnp.int32)[None, :]).astype(jnp.int32)
    before = jnp.cumsum(onehot, axis=0) - onehot
    return jnp.sum(before * onehot, axis=1)


def slot_table(targets, slot_count):
    wanted = targets[None, :] == jnp.arange(slot_count, dtype=jnp.int32)[:, None]
    picker = jnp.any(wanted.reshape(slot_count, -1, TOP), axis=2).astype(jnp.bfloat16)
    return (wanted, picker)


def fill_slots(picker, wanted, rows_in, rows_grad, route_probs):
    send_in = jnp.dot(picker, rows_in, preferred_element_type=jnp.float32).astype(jnp.bfloat16)
    send_grad = jnp.dot(picker, rows_grad, preferred_element_type=jnp.float32).astype(jnp.bfloat16)
    taken = jnp.where(wanted, route_probs.astype(jnp.float32)[None, :], jnp.zeros((), jnp.float32))
    send_prob = jnp.sum(taken, axis=1).astype(jnp.bfloat16)
    return (send_in, send_grad, send_prob)


def collect(picker, returned):
    flat = returned.reshape(picker.shape[0], -1)
    return lax.dot_general(
        picker, flat, (((0,), (0,)), ((), ())), preferred_element_type=jnp.float32
    )


def direct_plan(tokens, out_grad, expert_ids, probs, weights, capacity):
    n_dev = lax.axis_size(("group", "local"))
    width = tokens.shape[1]
    flat_ids = expert_ids.reshape(-1)
    targets = flat_ids * capacity + ranks_within(flat_ids, n_dev)
    wanted, picker = slot_table(targets, n_dev * capacity)
    send_in, send_grad, send_prob = fill_slots(picker, wanted, tokens, out_grad, probs.reshape(-1))
    rows_in = lax.all_to_all(
        send_in.reshape(n_dev, capacity, width),
        ("group", "local"),
        split_axis=0,
        concat_axis=0,
        tiled=True,
    )
    rows_grad = lax.all_to_all(
        send_grad.reshape(n_dev, capacity, width),
        ("group", "local"),
        split_axis=0,
        concat_axis=0,
        tiled=True,
    )
    rows_prob = lax.all_to_all(
        send_prob.reshape(n_dev, capacity),
        ("group", "local"),
        split_axis=0,
        concat_axis=0,
        tiled=True,
    )
    count = rows_in.shape[1]
    result = expert_backward(
        rows_in.reshape(-1, width),
        rows_grad.reshape(-1, width),
        rows_prob.reshape(-1),
        weights[0],
        weights[1],
        weights[2],
    )
    result = result.reshape(n_dev, count, width)
    returned = lax.all_to_all(result, ("group", "local"), split_axis=0, concat_axis=0, tiled=True)
    return collect(picker, returned).astype(jnp.bfloat16)


def local(tokens, out_grad, expert_ids, probs, w_gate, w_up, w_down):
    n_loc = lax.axis_size("local")
    per_group = TOP // GROUPS_TOKEN
    capacity = (per_group * tokens.shape[0] + n_loc - 1) // n_loc
    weights = (w_gate[0], w_up[0], w_down[0])
    return direct_plan(tokens, out_grad, expert_ids, probs, weights, capacity)


def solution(mesh):
    placed = (
        P(("group", "local"), None),
        P(("group", "local"), None),
        P(("group", "local"), None),
        P(("group", "local"), None),
        P(("group", "local"), None, None),
        P(("group", "local"), None, None),
        P(("group", "local"), None, None),
    )
    return jax.shard_map(
        local, mesh=mesh, in_specs=placed, out_specs=P(("group", "local"), None), check_vma=False
    )
```

profile of v0, /device:TPU:0, one launch (start us, length us, event | category | flops | bytes accessed | tf_op | source)
XLA Modules:
  0.0 159.6 jit_solution(2562255751697823400)
XLA Ops:
  0.0 0.8 copy.18
  0.8 0.1 eq.35
  0.9 0.8 copy.20
  1.6 0.1 reshape.76
  1.7 0.1 fusion.33
  1.8 0.2 reduce_window_sum.11
  2.0 0.2 select_reduce_fusion.1
  2.2 0.1 select_reduce_fusion
  2.3 0.8 convert_element_type.71
  3.1 11.1 %all-to-all-start = ((bf16[128,1,2]{2,1,0:T(2,128)(2,1)}), bf16[128,1,2]{2,1,0:T(2,128)(2,1)S(1)}, u32[]{:S(2)}, u32[]{:S(2)}) async-start(bf16[128,1,2]{2,1,0:T(2,128)(2,1)} %convert_element_type.71), calls=%async_computation | async-start | bytes 131072 | tf_op jit(solution)/shard_map/all_to_all | solution.py:71
  14.4 0.1 fusion.32
  14.5 0.7 convolution_convert_fusion
  15.2 1.7 %reshape.72 = bf16[128,2,3584]{2,1,0:T(2,128)(2,1)} reshape(bf16[256,3584]{1,0:T(8,128)(2,1)S(1)} %convolution_convert_fusion) | data formatting | bytes 3670016 | tf_op jit(solution)/shard_map/reshape | solution.py:58
  16.9 6.8 %all-to-all-done = bf16[128,1,2]{2,1,0:T(2,128)(2,1)S(1)} async-done(((bf16[128,1,2]{2,1,0:T(2,128)(2,1)}), bf16[128,1,2]{2,1,0:T(2,128)(2,1)S(1)}, u32[]{:S(2)}, u32[]{:S(2)}) %all-to-all-start) | async-done | bytes 544 | tf_op jit(solution)/shard_map/all_to_all | solution.py:71
  23.7 4.6 %all-to-all-start.2 = ((bf16[128,2,3584]{2,1,0:T(2,128)(2,1)}), bf16[128,2,3584]{2,1,0:T(2,128)(2,1)S(1)}, u32[]{:S(2)}, u32[]{:S(2)}) async-start(bf16[128,2,3584]{2,1,0:T(2,128)(2,1)} %reshape.72), calls=%async_computation.2 | async-start | bytes 3670016 | tf_op jit(solution)/shard_map/all_to_all | solution.py:57
  28.3 1.9 %convolution_convert_fusion.1 = bf16[256,3584]{1,0:T(8,128)(2,1)} fusion(pred[256,16]{0,1:T(8,128)(4,1)S(1)} %fusion.32, bf16[16,3584]{1,0:T(8,128)(2,1)S(1)} %copy-done.2), kind=kOutput, calls=%fused_computation.14 | convolution fusion | flops 30277632 | bytes 1953792 | tf_op jit(solution)/shard_map/dot_general | solution.py:37
  30.3 4.7 %reshape.70 = bf16[128,2,3584]{2,1,0:T(2,128)(2,1)} reshape(bf16[256,3584]{1,0:T(8,128)(2,1)} %convolution_convert_fusion.1) | data formatting | bytes 3670016 | tf_op jit(solution)/shard_map/reshape | solution.py:65
  35.0 20.4 %all-to-all-done.2 = bf16[128,2,3584]{2,1,0:T(2,128)(2,1)S(1)} async-done(((bf16[128,2,3584]{2,1,0:T(2,128)(2,1)}), bf16[128,2,3584]{2,1,0:T(2,128)(2,1)S(1)}, u32[]{:S(2)}, u32[]{:S(2)}) %all-to-all-start.2) | async-done | bytes 1835040 | tf_op jit(solution)/shard_map/all_to_all | solution.py:57
  55.4 5.9 %all-to-all-start.1 = ((bf16[128,2,3584]{2,1,0:T(2,128)(2,1)}), bf16[128,2,3584]{2,1,0:T(2,128)(2,1)}, u32[]{:S(2)}, u32[]{:S(2)}) async-start(bf16[128,2,3584]{2,1,0:T(2,128)(2,1)} %reshape.70), calls=%async_computation.1 | async-start | bytes 3670016 | tf_op jit(solution)/shard_map/all_to_all | solution.py:64
  61.3 0.2 convert_reduce_fusion
  61.5 0.1 reshape.77
  61.6 1.7 %reshape.73 = bf16[256,3584]{1,0:T(8,128)(2,1)} reshape(bf16[128,2,3584]{2,1,0:T(2,128)(2,1)S(1)} %all-to-all-done.2) | data formatting | bytes 3670016 | tf_op jit(solution)/shard_map/reshape | solution.py:80
  63.3 5.7 %fusion.2 = f32[256,1024]{1,0:T(8,128)S(1)} fusion(bf16[256,3584]{1,0:T(8,128)(2,1)} %reshape.73, bf16[1,3584,1024]{2,1,0:T(8,128)(2,1)} %param.11), kind=kOutput, calls=%fused_computation.2 | convolution fusion | flops 1879048192 | bytes 10223616 | tf_op jit(solution)/shard_map/dot_general | solution.py:11
  69.0 18.8 %all-to-all-done.1 = bf16[128,2,3584]{2,1,0:T(2,128)(2,1)} async-done(((bf16[128,2,3584]{2,1,0:T(2,128)(2,1)}), bf16[128,2,3584]{2,1,0:T(2,128)(2,1)}, u32[]{:S(2)}, u32[]{:S(2)}) %all-to-all-start.1) | async-done | bytes 1835040 | tf_op jit(solution)/shard_map/all_to_all | solution.py:64
  87.8 4.9 %reshape.71 = bf16[256,3584]{1,0:T(8,128)(2,1)} reshape(bf16[128,2,3584]{2,1,0:T(2,128)(2,1)} %all-to-all-done.1) | data formatting | bytes 3670016 | tf_op jit(solution)/shard_map/reshape | solution.py:81
  92.7 6.9 %fusion.8 = f32[256,1024]{1,0:T(8,128)} fusion(bf16[256,3584]{1,0:T(8,128)(2,1)} %reshape.71, bf16[1,1024,3584]{2,1,0:T(8,128)(2,1)} %param.13), kind=kOutput, calls=%fused_computation.8 | convolution fusion | flops 1879048192 | bytes 10223616 | tf_op jit(solution)/shard_map/dot_general | solution.py:14
  99.6 11.5 %fusion = f32[256,3584]{1,0:T(8,128)} fusion(bf16[1,3584,1024]{2,1,0:T(8,128)(2,1)} %param.11, f32[256,1024]{1,0:T(8,128)} %fusion.8, bf16[256,3584]{1,0:T(8,128)(2,1)S(1)} %copy-done.1, bf16[1,3584,1024]{2,1,0:T(8,128)(2,1)} %param.12, f32[256,1024]{1,0:T(8,128)S(1)} %fusion.2), kind=kOutput, calls=%fused_computation | convolution fusion | flops 3760717824 | bytes 22282240 | tf_op jit(solution)/shard_map/dot_general | solution.py:18
  111.1 7.8 %fusion.16 = bf16[256,3584]{1,0:T(8,128)(2,1)} fusion(f32[256,3584]{1,0:T(8,128)} %fusion, bf16[1,3584,1024]{2,1,0:T(8,128)(2,1)} %param.12, f32[256]{0:T(256)S(1)} %reshape.77, f32[256,1024]{1,0:T(8,128)} %fusion.8, f32[256,1024]{1,0:T(8,128)S(1)} %fusion.2), kind=kOutput, calls=%fused_computation.12 | convolution fusion | flops 1883373568 | bytes 14943232 | tf_op jit(solution)/shard_map/dot_general | solution.py:19
  118.9 3.9 %reshape.74 = bf16[128,2,3584]{2,1,0:T(2,128)(2,1)S(1)} reshape(bf16[256,3584]{1,0:T(8,128)(2,1)} %fusion.16) | data formatting | bytes 3670016 | tf_op jit(solution)/shard_map/reshape | solution.py:87
  122.8 31.7 %all_to_all.21 = bf16[128,2,3584]{2,1,0:T(2,128)(2,1)} all-to-all(bf16[128,2,3584]{2,1,0:T(2,128)(2,1)S(1)} %reshape.74), channel_id=1, replica_groups=mesh['group'=8,'local'=16] {'group','local'}, dimensions={0} | all-to-all | bytes 3670016 | tf_op jit(solution)/shard_map/all_to_all | solution.py:88
  154.5 4.1 %reshape.75 = bf16[256,3584]{1,0:T(8,128)(2,1)S(1)} reshape(bf16[128,2,3584]{2,1,0:T(2,128)(2,1)} %all_to_all.21) | data formatting | bytes 3670016 | tf_op jit(solution)/shard_map/reshape | solution.py:44
  158.6 1.0 convolution_convert_fusion.2
  (9 shorter events, 0.1 us)
Async XLA Ops:
  0.0 14.5 %copy-start = (bf16[16,3584]{1,0:T(8,128)(2,1)S(1)}, bf16[16,3584]{1,0:T(8,128)(2,1)}, u32[]{:S(2)}) copy-start(bf16[16,3584]{1,0:T(8,128)(2,1)} %param.7) | copy-start | bytes 344068
  3.1 20.6 %all-to-all-start = ((bf16[128,1,2]{2,1,0:T(2,128)(2,1)}), bf16[128,1,2]{2,1,0:T(2,128)(2,1)S(1)}, u32[]{:S(2)}, u32[]{:S(2)}) async-start(bf16[128,1,2]{2,1,0:T(2,128)(2,1)} %convert_element_type.71), calls=%async_computation | async-start | bytes 131072 | tf_op jit(solution)/shard_map/all_to_all | solution.py:71
  15.2 13.2 %copy-start.2 = (bf16[16,3584]{1,0:T(8,128)(2,1)S(1)}, bf16[16,3584]{1,0:T(8,128)(2,1)}, u32[]{:S(2)}) copy-start(bf16[16,3584]{1,0:T(8,128)(2,1)} %param.8) | copy-start | bytes 344068
  23.7 31.7 %all-to-all-start.2 = ((bf16[128,2,3584]{2,1,0:T(2,128)(2,1)}), bf16[128,2,3584]{2,1,0:T(2,128)(2,1)S(1)}, u32[]{:S(2)}, u32[]{:S(2)}) async-start(bf16[128,2,3584]{2,1,0:T(2,128)(2,1)} %reshape.72), calls=%async_computation.2 | async-start | bytes 3670016 | tf_op jit(solution)/shard_map/all_to_all | solution.py:57
  55.4 32.4 %all-to-all-start.1 = ((bf16[128,2,3584]{2,1,0:T(2,128)(2,1)}), bf16[128,2,3584]{2,1,0:T(2,128)(2,1)}, u32[]{:S(2)}, u32[]{:S(2)}) async-start(bf16[128,2,3584]{2,1,0:T(2,128)(2,1)} %reshape.70), calls=%async_computation.1 | async-start | bytes 3670016 | tf_op jit(solution)/shard_map/all_to_all | solution.py:64
  92.7 6.9 %copy-start.1 = (bf16[256,3584]{1,0:T(8,128)(2,1)S(1)}, bf16[256,3584]{1,0:T(8,128)(2,1)}, u32[]{:S(2)}) copy-start(bf16[256,3584]{1,0:T(8,128)(2,1)} %reshape.73) | copy-start | bytes 5505028
where the time goes:
time: 160 us
  waiting for transfers between devices  46 us (29%)
  matrix products  35.5 us (22%)
  blocking collectives  31.7 us (20%)
  local copies, waits for them, and re-layouts  23.7 us (15%)
  starting transfers between devices  21.7 us (14%)
    all_to_all x1, blocking collectives, direct_plan(): lax.all_to_all(result, ('group', 'local'), split_axis=0, concat_axis=0, t...  31.7 us
    all_to_all x1, waiting for transfers between devices, direct_plan(): lax.all_to_all(send_in.reshape(n_dev, capacity, width), ('group', 'local'...  20.4 us
    all_to_all x1, waiting for transfers between devices, direct_plan(): lax.all_to_all(send_grad.reshape(n_dev, capacity, width), ('group', 'loca...  18.8 us
    dot_general x1, matrix products, expert_backward(): lax.dot_general(d_gate, w_gate, contract, preferred_element_type=jnp.floa...  11.5 us
    all_to_all x1, starting transfers between devices, direct_plan(): lax.all_to_all(send_prob.reshape(n_dev, capacity), ('group', 'local'), sp...  11.1 us
    dot_general x1, matrix products, expert_backward(): lax.dot_general(d_up, w_up, contract, preferred_element_type=jnp.float32)  7.82 us
    dot_general x1, matrix products, expert_backward(): lax.dot_general(rows_grad, w_down, contract, preferred_element_type=jnp.f...  6.86 us
    all_to_all x1, waiting for transfers between devices, direct_plan(): lax.all_to_all(send_prob.reshape(n_dev, capacity), ('group', 'local'), sp...  6.79 us
  transfers between devices with their start and end apart: 3, of which 3 were waited for; matrix products, arithmetic and copies ran while one was open for 11% of the time, Pallas kernels for 0%

commit v1 on v0

v1 whole, which is shorter than its diff:
```python
import jax
import jax.numpy as jnp
from jax import lax
from jax.experimental import pallas as pl
from jax.experimental.pallas import tpu as pltpu
from jax.sharding import PartitionSpec as P

MESH = pl.DeviceIdType.MESH
D = 3584
F = 1024
TOK = 16
TILE = 128
THERE = ((4, 4, 4), (4, 3, 3), (2, 2, 2))
BACK = ((2, 2, 2), (4, 3, 3), (4, 4, 4))
NT = (((1,), (1,)), ((), ()))


def plan(waves):
    chunks, start = [], 0
    for wave in waves:
        row = []
        for kind, tiles in enumerate(wave):
            row.append((len(chunks) * 3 + kind, kind, start * TILE, tiles * TILE))
            start += tiles
        chunks.append(row)
    return chunks


def body(tokens, grads, ids, probs, w_gate, w_up, w_down, out, *scratch):
    there, back = plan(THERE), plan(BACK)
    n_there, n_back = 3 * len(THERE), 3 * len(BACK)
    scratch = list(scratch)

    def take(count):
        taken = scratch[:count]
        del scratch[:count]
        return taken

    x_buf, s_buf, g_buf = take(n_there), take(n_there), take(n_there)
    b_buf, r_buf, u_buf, ub_buf, v_buf, va_buf = (take(n_back) for _ in range(6))
    m_buf = take(3)
    p_buf, q_buf = take(3), take(3)
    to_first, from_first = take(2), take(2)
    tok_v, grad_v, ids_v, prob_v, wg_v, wu_v, wd_v = take(7)
    gate_acc, up_acc, hid_acc = take(3)
    dg_v, du_v = take(3), take(3)
    in_sem, send_sem, m_sem, xa_sem, xb_sem, xc_sem, rc_sem, rb_sem, ra_sem = take(9)

    group, local = lax.axis_index("group"), lax.axis_index("local")
    here = (group // 2, local // 4, local % 4)
    core = group % 2

    def device(axis, step, other):
        x, y, z = (lax.rem(c + (step if a == axis else 0), 4) for a, c in enumerate(here))
        k = lax.rem(core + other, 2)
        return (x * 2 + k, y * 4 + z)

    partners = [(axis, step, other) for axis in range(3) for step in (1, 2, 3) for other in (0, 1)]
    partners.append((0, 0, 1))
    barrier = pltpu.get_barrier_semaphore()
    for partner in partners:
        pl.semaphore_signal(barrier, inc=1, device_id=device(*partner), device_id_type=MESH)

    loads = [
        pltpu.make_async_copy(src, dst, in_sem.at[i])
        for i, (src, dst) in enumerate(
            (
                (ids, ids_v),
                (probs, prob_v),
                (tokens, tok_v),
                (grads, grad_v),
                (w_gate.at[0], wg_v),
                (w_up.at[0], wu_v),
                (w_down.at[0], wd_v),
            )
        )
    ]
    for load in loads:
        load.start()

    def send(src, dst, sem, recv, target):
        pltpu.make_async_remote_copy(
            src_ref=src,
            dst_ref=dst,
            send_sem=sem,
            recv_sem=recv,
            device_id=device(*target),
            device_id_type=MESH,
        ).start()

    def await_bytes(ref, sem):
        pltpu.make_async_copy(ref, ref, sem).wait()

    loads[0].wait()
    loads[1].wait()
    lane = lax.broadcasted_iota(jnp.int32, (TOK, 128), 1)
    dense = jnp.zeros((TOK, 128), jnp.float32)
    weight = prob_v[...].astype(jnp.float32)
    named = ids_v[...]
    for k in range(8):
        dense += jnp.where(named[:, k : k + 1] == lane, weight[:, k : k + 1], 0.0)
    earlier = lax.broadcasted_iota(jnp.int32, (TOK, TOK), 0) > lax.broadcasted_iota(jnp.int32, (TOK, TOK), 1)
    rank = jnp.dot(
        earlier.astype(jnp.bfloat16),
        (dense > 0.0).astype(jnp.bfloat16),
        preferred_element_type=jnp.float32,
    )
    meta = jnp.where(rank > 0.5, -dense, dense).astype(jnp.bfloat16)
    for kind in range(3):
        m_buf[kind][0:TOK] = meta
    def as_kind(row, kind):
        z, y, x = (jnp.bitwise_and(lax.shift_right_logical(row, shift), 3) for shift in (6, 3, 1))
        step = (x, y, z)
        moved = step[(kind + 2) % 3] * 64 + step[(kind + 1) % 3] * 8 + step[kind] * 2
        return moved + jnp.bitwise_and(row, 33)

    down = lax.broadcasted_iota(jnp.int32, (256, 256), 0)
    across = lax.broadcasted_iota(jnp.int32, (256, 256), 1)
    for kind in (1, 2):
        to_first[kind - 1][...] = (as_kind(down, kind) == across).astype(jnp.bfloat16)
        from_first[kind - 1][...] = (as_kind(across, kind) == down).astype(jnp.bfloat16)
    loads[2].wait()
    loads[3].wait()
    for row in there:
        for n, kind, start, width in row:
            x_buf[n][0, 0:TOK] = tok_v[:, start : start + width]
            x_buf[n][1, 0:TOK] = grad_v[:, start : start + width]

    pl.semaphore_wait(barrier, len(partners))

    for w, row in enumerate(there):
        for n, kind, start, width in row:
            for step in (2, 1, 3):
                rows = pl.ds(step * TOK, TOK)
                if w == 0:
                    send(
                        m_buf[kind].at[0:TOK], m_buf[kind].at[rows], send_sem.at[0], m_sem.at[kind], (kind, step, 0)
                    )
                send(
                    x_buf[n].at[:, 0:TOK], x_buf[n].at[:, rows], send_sem.at[1], xa_sem.at[n], (kind, step, 0)
                )

    for w, row in enumerate(there):
        for n, kind, start, width in row:
            second = (kind + 1) % 3
            if w == 0:
                await_bytes(m_buf[kind].at[TOK : 4 * TOK], m_sem.at[kind])
            await_bytes(x_buf[n].at[:, TOK : 4 * TOK], xa_sem.at[n])
            for step in (2, 1, 3):
                rows = pl.ds(step * 4 * TOK, 4 * TOK)
                if w == 0:
                    send(
                        m_buf[kind].at[0 : 4 * TOK],
                        m_buf[kind].at[rows],
                        send_sem.at[2],
                        m_sem.at[3 + kind],
                        (second, step, 0),
                    )
                send(
                    x_buf[n].at[:, 0 : 4 * TOK],
                    x_buf[n].at[:, rows],
                    send_sem.at[3],
                    xb_sem.at[n],
                    (second, step, 0),
                )

    def make_tables(kind):
        third = (kind + 2) % 3
        await_bytes(m_buf[kind].at[4 * TOK : 16 * TOK], m_sem.at[3 + kind])
        gathered = m_buf[kind][...]

        def expert(slot):
            block = lax.shift_right_logical(slot, 5)
            step = lax.shift_right_logical(block, 1)
            k = jnp.bitwise_and(core + jnp.bitwise_and(block, 1), 1)
            x, y, z = (jnp.bitwise_and(c + step, 3) if a == third else c for a, c in enumerate(here))
            return (x * 2 + k) * 16 + y * 4 + z

        def table(slot, token, found):
            source = jnp.bitwise_and(lax.shift_right_logical(slot, 1), 15)
            same = source == lax.shift_right_logical(token, 4)
            signed = jnp.where(jnp.bitwise_and(slot, 1) == 1, -found, found)
            return jnp.where(same & (signed > 0.0), signed, 0.0)

        def iota(shape, axis):
            return lax.broadcasted_iota(jnp.int32, shape, axis)

        picks = (iota((128, 256), 0) == expert(iota((128, 256), 1))).astype(jnp.bfloat16)
        found = jnp.dot(gathered, picks, preferred_element_type=jnp.float32)
        q_buf[kind][...] = table(iota((256, 256), 1), iota((256, 256), 0), found).astype(jnp.bfloat16)
        picks = (iota((256, 128), 1) == expert(iota((256, 128), 0))).astype(jnp.bfloat16)
        found = lax.dot_general(picks, gathered, NT, preferred_element_type=jnp.float32)
        taken = table(iota((256, 256), 0), iota((256, 256), 1), found)
        p_buf[kind][...] = (taken > 0.0).astype(jnp.bfloat16)

    def block(step, other):
        return pl.ds((step * 2 + other) * 32, 32)

    exchange = [(2, 0), (2, 1), (1, 0), (3, 0), (1, 1), (3, 1), (0, 1)]

    def pack(n, kind):
        third = (kind + 2) % 3
        await_bytes(x_buf[n].at[:, 4 * TOK : 16 * TOK], xb_sem.at[n])
        for half in range(2):
            rows = jnp.dot(p_buf[kind][...], x_buf[n][half], preferred_element_type=jnp.float32).astype(jnp.bfloat16)
            g_buf[n][half, 0:32] = rows[0:32]
            s_buf[n][half] = rows
        for step, other in exchange:
            send(
                s_buf[n].at[:, block(step, other)],
                g_buf[n].at[:, block(step, other)],
                send_sem.at[4],
                xc_sem.at[n],
                (third, step, other),
            )

    def absorb(n, kind, start, width, first):
        await_bytes(g_buf[n].at[:, 32:256], xc_sem.at[n])
        if kind:
            for half in range(2):
                g_buf[n][half] = jnp.dot(
                    to_first[kind - 1][...], g_buf[n][half], preferred_element_type=jnp.float32
                ).astype(jnp.bfloat16)

        def columns(i, carry):
            cols = pl.ds(pl.multiple_of(i * 256, 256), 256)
            rows_in, rows_grad = g_buf[n][0], g_buf[n][1]
            gate = jnp.dot(rows_in, wg_v[start : start + width, cols], preferred_element_type=jnp.float32)
            upward = jnp.dot(rows_in, wu_v[start : start + width, cols], preferred_element_type=jnp.float32)
            hidden = lax.dot_general(
                rows_grad, wd_v[cols, start : start + width], NT, preferred_element_type=jnp.float32
            )
            if first:
                gate_acc[:, cols] = gate
                up_acc[:, cols] = upward
                hid_acc[:, cols] = hidden
            else:
                gate_acc[:, cols] += gate
                up_acc[:, cols] += upward
                hid_acc[:, cols] += hidden
            return carry

        lax.fori_loop(0, F // 256, columns, 0)

    def absorb_wave(w):
        if w == 0:
            for load in loads[4:]:
                load.wait()
        for n, kind, start, width in there[w]:
            absorb(n, kind, start, width, n == 0)

    for w, row in enumerate(there):
        for n, kind, start, width in row:
            if w == 0:
                make_tables(kind)
            pack(n, kind)
        if w >= 1:
            absorb_wave(w - 1)
    absorb_wave(len(there) - 1)

    def middle(i, carry):
        cols = pl.ds(pl.multiple_of(i * 256, 256), 256)
        gate, upward, hidden = gate_acc[:, cols], up_acc[:, cols], hid_acc[:, cols]
        s = jax.nn.sigmoid(gate)
        d_gate = (hidden * upward * (s * (1.0 + gate * (1.0 - s)))).astype(jnp.bfloat16)
        d_up = (hidden * (gate * s)).astype(jnp.bfloat16)
        dg_v[0][:, cols] = d_gate
        du_v[0][:, cols] = d_up
        for kind in (1, 2):
            order = from_first[kind - 1][...]
            dg_v[kind][:, cols] = jnp.dot(order, d_gate, preferred_element_type=jnp.float32).astype(jnp.bfloat16)
            du_v[kind][:, cols] = jnp.dot(order, d_up, preferred_element_type=jnp.float32).astype(jnp.bfloat16)
        return carry

    lax.fori_loop(0, F // 256, middle, 0)

    def give(n, kind, start, width):
        third = (kind + 2) % 3
        result = lax.dot_general(dg_v[kind][...], wg_v[start : start + width], NT, preferred_element_type=jnp.float32)
        result += lax.dot_general(du_v[kind][...], wu_v[start : start + width], NT, preferred_element_type=jnp.float32)
        result = result.astype(jnp.bfloat16)
        r_buf[n][0:32] = result[0:32]
        b_buf[n][...] = result
        for step, other in exchange:
            send(
                b_buf[n].at[block(step, other)],
                r_buf[n].at[block(step, other)],
                send_sem.at[5],
                rc_sem.at[n],
                (third, (4 - step) % 4, other),
            )

    def combine(n, kind):
        second = (kind + 1) % 3
        await_bytes(r_buf[n].at[32:256], rc_sem.at[n])
        part = jnp.dot(q_buf[kind][...], r_buf[n][...], preferred_element_type=jnp.float32)
        u_buf[n][...] = part.astype(jnp.bfloat16)
        for step in (2, 1, 3):
            send(
                u_buf[n].at[pl.ds(step * 64, 64)],
                ub_buf[n].at[pl.ds(step * 64, 64)],
                send_sem.at[6],
                rb_sem.at[n],
                (second, 4 - step, 0),
            )

    def reduce_second(n, kind):
        await_bytes(ub_buf[n].at[64:256], rb_sem.at[n])
        part = u_buf[n][0:64].astype(jnp.float32)
        for step in (1, 2, 3):
            part += ub_buf[n][step * 64 : step * 64 + 64].astype(jnp.float32)
        v_buf[n][...] = part.astype(jnp.bfloat16)
        for step in (2, 1, 3):
            send(
                v_buf[n].at[pl.ds(step * TOK, TOK)],
                va_buf[n].at[pl.ds(step * TOK, TOK)],
                send_sem.at[7],
                ra_sem.at[n],
                (kind, 4 - step, 0),
            )

    def finish(n, start, width):
        await_bytes(va_buf[n].at[TOK : 4 * TOK], ra_sem.at[n])
        part = v_buf[n][0:TOK].astype(jnp.float32)
        for step in (1, 2, 3):
            part += va_buf[n][step * TOK : step * TOK + TOK].astype(jnp.float32)
        out[:, start : start + width] = part.astype(jnp.bfloat16)

    waves = len(back)
    for w in range(waves):
        for n, kind, start, width in back[w]:
            give(n, kind, start, width)
    for w in range(waves + 2):
        if w < waves:
            for n, kind, start, width in back[w]:
                combine(n, kind)
        if 1 <= w <= waves:
            for n, kind, start, width in back[w - 1]:
                reduce_second(n, kind)
        if w >= 2:
            for n, kind, start, width in back[w - 2]:
                finish(n, start, width)

    for row in there:
        for n, kind, start, width in row:
            if n < 3:
                await_bytes(m_buf[kind].at[0 : 3 * TOK], send_sem.at[0])
                await_bytes(m_buf[kind].at[0 : 12 * TOK], send_sem.at[2])
            await_bytes(x_buf[n].at[:, 0 : 3 * TOK], send_sem.at[1])
            await_bytes(x_buf[n].at[:, 0 : 12 * TOK], send_sem.at[3])
            await_bytes(s_buf[n].at[:, 32:256], send_sem.at[4])
    for row in back:
        for n, kind, start, width in row:
            await_bytes(b_buf[n].at[32:256], send_sem.at[5])
            await_bytes(u_buf[n].at[64:256], send_sem.at[6])
            await_bytes(v_buf[n].at[TOK : 4 * TOK], send_sem.at[7])


def local_part(tokens, out_grad, expert_ids, probs, w_gate, w_up, w_down):
    there = [c[3] for row in plan(THERE) for c in row]
    back = [c[3] for row in plan(BACK) for c in row]
    bf16, f32 = jnp.bfloat16, jnp.float32
    scratch = (
        [pltpu.VMEM((2, 256, w), bf16) for _ in range(3) for w in there]
        + [pltpu.VMEM((256, w), bf16) for _ in range(4) for w in back]
        + [pltpu.VMEM((64, w), bf16) for _ in range(2) for w in back]
        + [pltpu.VMEM((256, 128), bf16)] * 3
        + [pltpu.VMEM((256, 256), bf16)] * 10
        + [
            pltpu.VMEM((TOK, D), bf16),
            pltpu.VMEM((TOK, D), bf16),
            pltpu.VMEM((TOK, 8), jnp.int32),
            pltpu.VMEM((TOK, 8), bf16),
            pltpu.VMEM((D, F), bf16),
            pltpu.VMEM((D, F), bf16),
            pltpu.VMEM((F, D), bf16),
        ]
        + [pltpu.VMEM((256, F), f32)] * 3
        + [pltpu.VMEM((256, F), bf16)] * 6
        + [
            pltpu.SemaphoreType.DMA((7,)),
            pltpu.SemaphoreType.DMA((8,)),
            pltpu.SemaphoreType.DMA((6,)),
            pltpu.SemaphoreType.DMA((len(there),)),
            pltpu.SemaphoreType.DMA((len(there),)),
            pltpu.SemaphoreType.DMA((len(there),)),
            pltpu.SemaphoreType.DMA((len(back),)),
            pltpu.SemaphoreType.DMA((len(back),)),
            pltpu.SemaphoreType.DMA((len(back),)),
        ]
    )
    return pl.pallas_call(
        body,
        out_shape=jax.ShapeDtypeStruct((TOK, D), bf16),
        in_specs=[pl.BlockSpec(memory_space=pl.ANY)] * 7,
        out_specs=pl.BlockSpec(memory_space=pltpu.VMEM),
        scratch_shapes=scratch,
        compiler_params=pltpu.CompilerParams(
            collective_id=0, has_side_effects=True, vmem_limit_bytes=60 * 1024 * 1024
        ),
        cost_estimate=pl.CostEstimate(flops=2 * 256 * D * F * 5, bytes_accessed=3 * D * F * 2, transcendentals=256 * F),
    )(tokens, out_grad, expert_ids, probs, w_gate, w_up, w_down)


def solution(mesh):
    flat = P(("group", "local"), None)
    deep = P(("group", "local"), None, None)
    return jax.shard_map(
        local_part,
        mesh=mesh,
        in_specs=(flat, flat, flat, flat, deep, deep, deep),
        out_specs=flat,
        check_vma=False,
    )
```

time: 160 us -> 82.9 us (0.52)
  Pallas kernels: 0 us -> 78.4 us
  waiting for transfers between devices: 46 us -> 0 us
  matrix products: 35.5 us -> 0 us
  blocking collectives: 31.7 us -> 0 us
  starting transfers between devices: 21.7 us -> 0 us
  local copies, waits for them, and re-layouts: 23.7 us -> 4.25 us
    pallas_call x0 -> x1, Pallas kernels: none -> 78.4 us  [local_part(): pl.pallas_call(body, out_shape=jax.ShapeDtypeStruct((TOK, D), bf16), in_s...]
    all_to_all x3 -> x0, waiting for transfers between devices: 46 us -> none  [the longest x1 20.4 us: direct_plan(): lax.all_to_all(send_in.reshape(n_dev, capacity, width), ('group', 'local'...]
    dot_general x7 -> x0, matrix products: 35.5 us -> none  [the longest x1 11.5 us: expert_backward(): lax.dot_general(d_gate, w_gate, contract, preferred_element_type=jnp.floa...]
    all_to_all x1 -> x0, blocking collectives: 31.7 us -> none  [direct_plan(): lax.all_to_all(result, ('group', 'local'), split_axis=0, concat_axis=0, t...]
    all_to_all x3 -> x0, starting transfers between devices: 21.7 us -> none  [the longest x1 11.1 us: direct_plan(): lax.all_to_all(send_prob.reshape(n_dev, capacity), ('group', 'local'), sp...]
    reshape x6 -> x0, local copies, waits for them, and re-layouts: 21 us -> none  [the longest x1 4.91 us: direct_plan(): rows_grad.reshape(-1, width)]
    unnamed x7 -> x3, local copies, waits for them, and re-layouts: 0.81 us -> 4.25 us
    convert_element_type x4 -> x0, local copies, waits for them, and re-layouts: 1.79 us -> none  [the longest x2 0.84 us: fill_slots(): route_probs.astype(jnp.float32)[None, :]]
  transfers between devices with their start and end apart: 3 -> 0, of which waited for: 3 -> 0; matrix products, arithmetic and copies ran while one was open for 11% -> 0% of each run, Pallas kernels for 0% -> 0%
where the time goes in v1:
time: 82.9 us; the launch traced here: 82.7 us
  Pallas kernels  78.4 us (95%)
  local copies, waits for them, and re-layouts  4.25 us (5%)
    pallas_call x1, Pallas kernels, local_part(): pl.pallas_call(body, out_shape=jax.ShapeDtypeStruct((TOK, D), bf16), in_s...  78.4 us
    unnamed x3, local copies, waits for them, and re-layouts  4.25 us

profile of v1, /device:TPU:0, one launch (start us, length us, event | category | flops | bytes accessed | tf_op | source)
XLA Modules:
  0.0 82.7 jit_solution(16691071826158579719)
XLA Ops:
  0.0 1.3 %copy.9.probs = bf16[16,8]{1,0:T(8,128)(2,1)} copy(bf16[16,8]{0,1:T(8,128)(2,1)} %param.10) | data formatting | bytes 512 | tf_op args[3]
  1.3 1.4 %copy.8.ids = s32[16,8]{1,0:T(8,128)} copy(s32[16,8]{0,1:T(8,128)} %param.9) | data formatting | bytes 1024 | tf_op args[2]
  2.7 78.4 %shard_map.73 = bf16[16,3584]{1,0:T(8,128)(2,1)} custom-call(bf16[16,3584]{1,0:T(8,128)(2,1)} %tokens.1, bf16[16,3584]{1,0:T(8,128)(2,1)} %grads.1, s32[16,8]{1,0:T(8,128)} %copy.8.ids, bf16[16,8]{1,0:T(8,128)(2,1)} %copy.9.probs, bf16[1,3584,1024]{2,1,0:T(8,128)(2,1)} %w_gate.1, bf16[1,3584,1024]{2,1,0:T(8,128)(2,1)} %w_up.1, bf16[1,1024,3584]{2,1,0:T(8,128)(2,1)} %w_down.1), custom_call_target="tpu_custom_call" | custom-call | flops 9395240960 | bytes 22020096 | tf_op jit(solution)/shard_map/pallas_call | solution.py:392
  81.1 1.6 %copy.11 = bf16[16,3584]{1,0:T(8,128)(2,1)} copy(bf16[16,3584]{1,0:T(8,128)(2,1)} %shard_map.73) | data formatting | bytes 229376

commit v2 on v1

--- a/solution.py
+++ b/solution.py
@@ -11,7 +11,9 @@
 TOK = 16
 TILE = 128
 THERE = ((4, 4, 4), (4, 3, 3), (2, 2, 2))
-BACK = ((2, 2, 2), (4, 3, 3), (4, 4, 4))
+BACK = ((4, 4, 4), (4, 3, 3), (2, 2, 2))
+N_STEP = 512
+LAST_STEP = 256
 NT = (((1,), (1,)), ((), ()))
 
 
@@ -36,15 +38,15 @@
         del scratch[:count]
         return taken
 
-    x_buf, s_buf, g_buf = take(n_there), take(n_there), take(n_there)
+    x_buf, s_buf, g_buf = take(n_there), take(n_there), take(len(THERE))
     b_buf, r_buf, u_buf, ub_buf, v_buf, va_buf = (take(n_back) for _ in range(6))
     m_buf = take(3)
     p_buf, q_buf = take(3), take(3)
     to_first, from_first = take(2), take(2)
-    tok_v, grad_v, ids_v, prob_v, wg_v, wu_v, wd_v = take(7)
+    ids_v, prob_v, wg_v, wu_v, wd_v = take(5)
     gate_acc, up_acc, hid_acc = take(3)
     dg_v, du_v = take(3), take(3)
-    in_sem, send_sem, m_sem, xa_sem, xb_sem, xc_sem, rc_sem, rb_sem, ra_sem = take(9)
+    in_sem, x_sem, send_sem, m_sem, xa_sem, xb_sem, xc_sem, rc_sem, rb_sem, ra_sem = take(10)
 
     group, local = lax.axis_index("group"), lax.axis_index("local")
     here = (group // 2, local // 4, local % 4)
@@ -61,22 +63,19 @@
     for partner in partners:
         pl.semaphore_signal(barrier, inc=1, device_id=device(*partner), device_id_type=MESH)
 
-    loads = [
-        pltpu.make_async_copy(src, dst, in_sem.at[i])
-        for i, (src, dst) in enumerate(
-            (
-                (ids, ids_v),
-                (probs, prob_v),
-                (tokens, tok_v),
-                (grads, grad_v),
-                (w_gate.at[0], wg_v),
-                (w_up.at[0], wu_v),
-                (w_down.at[0], wd_v),
-            )
-        )
-    ]
-    for load in loads:
-        load.start()
+    loads = []
+
+    def load(src, dst, sem):
+        loads.append(pltpu.make_async_copy(src, dst, sem))
+        loads[-1].start()
+
+    for row in there:
+        for n, kind, start, width in row:
+            cols = slice(start, start + width)
+            load(tokens.at[:, cols], x_buf[n].at[0, 0:TOK], x_sem.at[0, n])
+            load(grads.at[:, cols], x_buf[n].at[1, 0:TOK], x_sem.at[1, n])
+    load(ids, ids_v, in_sem.at[0])
+    load(probs, prob_v, in_sem.at[1])
 
     def send(src, dst, sem, recv, target):
         pltpu.make_async_remote_copy(
@@ -91,12 +90,32 @@
     def await_bytes(ref, sem):
         pltpu.make_async_copy(ref, ref, sem).wait()
 
-    loads[0].wait()
-    loads[1].wait()
+    for copy in loads[: 2 * n_there]:
+        copy.wait()
+    pl.semaphore_wait(barrier, len(partners))
+
+    for row in there:
+        for n, kind, start, width in row:
+            for step in (2, 1, 3):
+                send(
+                    x_buf[n].at[:, 0:TOK],
+                    x_buf[n].at[:, pl.ds(step * TOK, TOK)],
+                    send_sem.at[1],
+                    xa_sem.at[n],
+                    (kind, step, 0),
+                )
+
+    for copy in loads[2 * n_there : 2 * n_there + 2]:
+        copy.wait()
     lane = lax.broadcasted_iota(jnp.int32, (TOK, 128), 1)
     dense = jnp.zeros((TOK, 128), jnp.float32)
-    weight = prob_v[...].astype(jnp.float32)
-    named = ids_v[...]
+    same = (
+        lax.broadcasted_iota(jnp.int32, (TOK, TOK), 0) == lax.broadcasted_iota(jnp.int32, (TOK, TOK), 1)
+    ).astype(jnp.bfloat16)
+    weight = lax.dot_general(same, prob_v[...], NT, preferred_element_type=jnp.float32)
+    named = lax.dot_general(
+        same, ids_v[...].astype(jnp.bfloat16), NT, preferred_element_type=jnp.float32
+    ).astype(jnp.int32)
     for k in range(8):
         dense += jnp.where(named[:, k : k + 1] == lane, weight[:, k : k + 1], 0.0)
     earlier = lax.broadcasted_iota(jnp.int32, (TOK, TOK), 0) > lax.broadcasted_iota(jnp.int32, (TOK, TOK), 1)
@@ -108,6 +127,13 @@
     meta = jnp.where(rank > 0.5, -dense, dense).astype(jnp.bfloat16)
     for kind in range(3):
         m_buf[kind][0:TOK] = meta
+    for kind in range(3):
+        for step in (2, 1, 3):
+            rows = pl.ds(step * TOK, TOK)
+            send(m_buf[kind].at[0:TOK], m_buf[kind].at[rows], send_sem.at[0], m_sem.at[kind], (kind, step, 0))
+    for src, dst, sem in ((w_gate, wg_v, 2), (w_up, wu_v, 3), (w_down, wd_v, 4)):
+        load(src.at[0], dst, in_sem.at[sem])
+
     def as_kind(row, kind):
         z, y, x = (jnp.bitwise_and(lax.shift_right_logical(row, shift), 3) for shift in (6, 3, 1))
         step = (x, y, z)
@@ -119,27 +145,6 @@
     for kind in (1, 2):
         to_first[kind - 1][...] = (as_kind(down, kind) == across).astype(jnp.bfloat16)
         from_first[kind - 1][...] = (as_kind(across, kind) == down).astype(jnp.bfloat16)
-    loads[2].wait()
-    loads[3].wait()
-    for row in there:
-        for n, kind, start, width in row:
-            x_buf[n][0, 0:TOK] = tok_v[:, start : start + width]
-            x_buf[n][1, 0:TOK] = grad_v[:, start : start + width]
-
-    pl.semaphore_wait(barrier, len(partners))
-
-    for w, row in enumerate(there):
-        for n, kind, start, width in row:
-            for step in (2, 1, 3):
-                rows = pl.ds(step * TOK, TOK)
-                if w == 0:
-                    send(
-                        m_buf[kind].at[0:TOK], m_buf[kind].at[rows], send_sem.at[0], m_sem.at[kind], (kind, step, 0)
-                    )
-                send(
-                    x_buf[n].at[:, 0:TOK], x_buf[n].at[:, rows], send_sem.at[1], xa_sem.at[n], (kind, step, 0)
-                )
-
     for w, row in enumerate(there):
         for n, kind, start, width in row:
             second = (kind + 1) % 3
@@ -157,11 +162,7 @@
                         (second, step, 0),
                     )
                 send(
-                    x_buf[n].at[:, 0 : 4 * TOK],
-                    x_buf[n].at[:, rows],
-                    send_sem.at[3],
-                    xb_sem.at[n],
-                    (second, step, 0),
+                    x_buf[n].at[:, 0 : 4 * TOK], x_buf[n].at[:, rows], send_sem.at[3], xb_sem.at[n], (second, step, 0)
                 )
 
     def make_tables(kind):
@@ -198,84 +199,87 @@
 
     exchange = [(2, 0), (2, 1), (1, 0), (3, 0), (1, 1), (3, 1), (0, 1)]
 
-    def pack(n, kind):
+    def landing(w, n, start, width):
+        at = start - there[w][0][2]
+        return g_buf[w].at[:, :, at : at + width]
+
+    def pack(w, n, kind, start, width):
         third = (kind + 2) % 3
         await_bytes(x_buf[n].at[:, 4 * TOK : 16 * TOK], xb_sem.at[n])
+        land = landing(w, n, start, width)
         for half in range(2):
             rows = jnp.dot(p_buf[kind][...], x_buf[n][half], preferred_element_type=jnp.float32).astype(jnp.bfloat16)
-            g_buf[n][half, 0:32] = rows[0:32]
+            land[half, 0:32] = rows[0:32]
             s_buf[n][half] = rows
         for step, other in exchange:
             send(
                 s_buf[n].at[:, block(step, other)],
-                g_buf[n].at[:, block(step, other)],
+                land.at[:, block(step, other)],
                 send_sem.at[4],
                 xc_sem.at[n],
                 (third, step, other),
             )
 
-    def absorb(n, kind, start, width, first):
-        await_bytes(g_buf[n].at[:, 32:256], xc_sem.at[n])
-        if kind:
-            for half in range(2):
-                g_buf[n][half] = jnp.dot(
-                    to_first[kind - 1][...], g_buf[n][half], preferred_element_type=jnp.float32
-                ).astype(jnp.bfloat16)
-
-        def columns(i, carry):
-            cols = pl.ds(pl.multiple_of(i * 256, 256), 256)
-            rows_in, rows_grad = g_buf[n][0], g_buf[n][1]
-            gate = jnp.dot(rows_in, wg_v[start : start + width, cols], preferred_element_type=jnp.float32)
-            upward = jnp.dot(rows_in, wu_v[start : start + width, cols], preferred_element_type=jnp.float32)
+    def absorb(w):
+        if w == 0:
+            for copy in loads[2 * n_there + 2 :]:
+                copy.wait()
+        for n, kind, start, width in there[w]:
+            land = landing(w, n, start, width)
+            await_bytes(land.at[:, 32:256], xc_sem.at[n])
+            if kind:
+                for half in range(2):
+                    land[half] = jnp.dot(
+                        to_first[kind - 1][...], land[half], preferred_element_type=jnp.float32
+                    ).astype(jnp.bfloat16)
+        first, span = there[w][0][2], sum(THERE[w]) * TILE
+
+        def columns(cols):
+            rows_in, rows_grad = g_buf[w][0], g_buf[w][1]
+            gate = jnp.dot(rows_in, wg_v[first : first + span, cols], preferred_element_type=jnp.float32)
+            upward = jnp.dot(rows_in, wu_v[first : first + span, cols], preferred_element_type=jnp.float32)
             hidden = lax.dot_general(
-                rows_grad, wd_v[cols, start : start + width], NT, preferred_element_type=jnp.float32
+                rows_grad, wd_v[cols, first : first + span], NT, preferred_element_type=jnp.float32
             )
-            if first:
-                gate_acc[:, cols] = gate
-                up_acc[:, cols] = upward
-                hid_acc[:, cols] = hidden
-            else:
-                gate_acc[:, cols] += gate
-                up_acc[:, cols] += upward
-                hid_acc[:, cols] += hidden
+            if w > 0:
+                gate += gate_acc[:, cols]
+                upward += up_acc[:, cols]
+                hidden += hid_acc[:, cols]
+            return gate, upward, hidden
+
+        def store(i, carry):
+            cols = pl.ds(pl.multiple_of(i * N_STEP, N_STEP), N_STEP)
+            gate_acc[:, cols], up_acc[:, cols], hid_acc[:, cols] = columns(cols)
             return carry
 
-        lax.fori_loop(0, F // 256, columns, 0)
-
-    def absorb_wave(w):
-        if w == 0:
-            for load in loads[4:]:
-                load.wait()
-        for n, kind, start, width in there[w]:
-            absorb(n, kind, start, width, n == 0)
+        if w < len(there) - 1:
+            lax.fori_loop(0, F // N_STEP, store, 0)
+            return
+        for at in range(0, F, LAST_STEP):
+            cols = slice(at, at + LAST_STEP)
+            gate, upward, hidden = columns(cols)
+            s = jax.nn.sigmoid(gate)
+            dg_v[0][:, cols] = (hidden * upward * (s * (1.0 + gate * (1.0 - s)))).astype(jnp.bfloat16)
+            du_v[0][:, cols] = (hidden * (gate * s)).astype(jnp.bfloat16)
 
     for w, row in enumerate(there):
         for n, kind, start, width in row:
             if w == 0:
                 make_tables(kind)
-            pack(n, kind)
+            pack(w, n, kind, start, width)
         if w >= 1:
-            absorb_wave(w - 1)
-    absorb_wave(len(there) - 1)
-
-    def middle(i, carry):
-        cols = pl.ds(pl.multiple_of(i * 256, 256), 256)
-        gate, upward, hidden = gate_acc[:, cols], up_acc[:, cols], hid_acc[:, cols]
-        s = jax.nn.sigmoid(gate)
-        d_gate = (hidden * upward * (s * (1.0 + gate * (1.0 - s)))).astype(jnp.bfloat16)
-        d_up = (hidden * (gate * s)).astype(jnp.bfloat16)
-        dg_v[0][:, cols] = d_gate
-        du_v[0][:, cols] = d_up
-        for kind in (1, 2):
-            order = from_first[kind - 1][...]
-            dg_v[kind][:, cols] = jnp.dot(order, d_gate, preferred_element_type=jnp.float32).astype(jnp.bfloat16)
-            du_v[kind][:, cols] = jnp.dot(order, d_up, preferred_element_type=jnp.float32).astype(jnp.bfloat16)
-        return carry
-
-    lax.fori_loop(0, F // 256, middle, 0)
+            absorb(w - 1)
+    absorb(len(there) - 1)
+
+    def reorder(kind):
+        order = from_first[kind - 1][...]
+        for held in (dg_v, du_v):
+            held[kind][...] = jnp.dot(order, held[0][...], preferred_element_type=jnp.float32).astype(jnp.bfloat16)
 
     def give(n, kind, start, width):
         third = (kind + 2) % 3
+        if 0 < n < 3:
+            reorder(kind)
         result = lax.dot_general(dg_v[kind][...], wg_v[start : start + width], NT, preferred_element_type=jnp.float32)
         result += lax.dot_general(du_v[kind][...], wu_v[start : start + width], NT, preferred_element_type=jnp.float32)
         result = result.astype(jnp.bfloat16)
@@ -296,13 +300,8 @@
         part = jnp.dot(q_buf[kind][...], r_buf[n][...], preferred_element_type=jnp.float32)
         u_buf[n][...] = part.astype(jnp.bfloat16)
         for step in (2, 1, 3):
-            send(
-                u_buf[n].at[pl.ds(step * 64, 64)],
-                ub_buf[n].at[pl.ds(step * 64, 64)],
-                send_sem.at[6],
-                rb_sem.at[n],
-                (second, 4 - step, 0),
-            )
+            rows = pl.ds(step * 64, 64)
+            send(u_buf[n].at[rows], ub_buf[n].at[rows], send_sem.at[6], rb_sem.at[n], (second, 4 - step, 0))
 
     def reduce_second(n, kind):
         await_bytes(ub_buf[n].at[64:256], rb_sem.at[n])
@@ -324,21 +323,21 @@
         part = v_buf[n][0:TOK].astype(jnp.float32)
         for step in (1, 2, 3):
             part += va_buf[n][step * TOK : step * TOK + TOK].astype(jnp.float32)
-        out[:, start : start + width] = part.astype(jnp.bfloat16)
+        out[:, start : start + width] = part
 
     waves = len(back)
-    for w in range(waves):
-        for n, kind, start, width in back[w]:
-            give(n, kind, start, width)
-    for w in range(waves + 2):
+    for w in range(waves + 3):
         if w < waves:
             for n, kind, start, width in back[w]:
-                combine(n, kind)
+                give(n, kind, start, width)
         if 1 <= w <= waves:
             for n, kind, start, width in back[w - 1]:
+                combine(n, kind)
+        if 2 <= w <= waves + 1:
+            for n, kind, start, width in back[w - 2]:
                 reduce_second(n, kind)
-        if w >= 2:
-            for n, kind, start, width in back[w - 2]:
+        if w >= 3:
+            for n, kind, start, width in back[w - 3]:
                 finish(n, start, width)
 
     for row in there:
@@ -361,16 +360,15 @@
     back = [c[3] for row in plan(BACK) for c in row]
     bf16, f32 = jnp.bfloat16, jnp.float32
     scratch = (
-        [pltpu.VMEM((2, 256, w), bf16) for _ in range(3) for w in there]
+        [pltpu.VMEM((2, 256, w), bf16) for _ in range(2) for w in there]
+        + [pltpu.VMEM((2, 256, sum(wave) * TILE), bf16) for wave in THERE]
         + [pltpu.VMEM((256, w), bf16) for _ in range(4) for w in back]
         + [pltpu.VMEM((64, w), bf16) for _ in range(2) for w in back]
         + [pltpu.VMEM((256, 128), bf16)] * 3
         + [pltpu.VMEM((256, 256), bf16)] * 10
         + [
-            pltpu.VMEM((TOK, D), bf16),
-            pltpu.VMEM((TOK, D), bf16),
-            pltpu.VMEM((TOK, 8), jnp.int32),
-            pltpu.VMEM((TOK, 8), bf16),
+            pltpu.VMEM((8, TOK), jnp.int32),
+            pltpu.VMEM((8, TOK), bf16),
             pltpu.VMEM((D, F), bf16),
             pltpu.VMEM((D, F), bf16),
             pltpu.VMEM((F, D), bf16),
@@ -378,7 +376,8 @@
         + [pltpu.VMEM((256, F), f32)] * 3
         + [pltpu.VMEM((256, F), bf16)] * 6
         + [
-            pltpu.SemaphoreType.DMA((7,)),
+            pltpu.SemaphoreType.DMA((5,)),
+            pltpu.SemaphoreType.DMA((2, len(there))),
             pltpu.SemaphoreType.DMA((8,)),
             pltpu.SemaphoreType.DMA((6,)),
             pltpu.SemaphoreType.DMA((len(there),)),
@@ -389,9 +388,9 @@
             pltpu.SemaphoreType.DMA((len(back),)),
         ]
     )
-    return pl.pallas_call(
+    total = pl.pallas_call(
         body,
-        out_shape=jax.ShapeDtypeStruct((TOK, D), bf16),
+        out_shape=jax.ShapeDtypeStruct((TOK, D), f32),
         in_specs=[pl.BlockSpec(memory_space=pl.ANY)] * 7,
         out_specs=pl.BlockSpec(memory_space=pltpu.VMEM),
         scratch_shapes=scratch,
@@ -399,7 +398,8 @@
             collective_id=0, has_side_effects=True, vmem_limit_bytes=60 * 1024 * 1024
         ),
         cost_estimate=pl.CostEstimate(flops=2 * 256 * D * F * 5, bytes_accessed=3 * D * F * 2, transcendentals=256 * F),
-    )(tokens, out_grad, expert_ids, probs, w_gate, w_up, w_down)
+    )(tokens, out_grad, expert_ids.T, probs.T, w_gate, w_up, w_down)
+    return total.astype(bf16)
 
 
 def solution(mesh):

time: 82.9 us -> 74.2 us (0.90)
  Pallas kernels: 78.4 us -> 72.4 us
  local copies, waits for them, and re-layouts: 4.25 us -> 0 us
  other arithmetic: 0 us -> 1.6 us
    pallas_call x1, Pallas kernels: 78.4 us -> 72.4 us  [local_part(): pl.pallas_call(body, out_shape=jax.ShapeDtypeStruct((TOK, D), f32), in_sp...]
    unnamed x3 -> x0, local copies, waits for them, and re-layouts: 4.25 us -> none
    convert_element_type x0 -> x1, other arithmetic: none -> 1.6 us  [local_part(): return total.astype(bf16)]
where the time goes in v2:
time: 74.2 us; the launch traced here: 74 us
  Pallas kernels  72.4 us (98%)
  other arithmetic  1.6 us (2%)
    pallas_call x1, Pallas kernels, local_part(): pl.pallas_call(body, out_shape=jax.ShapeDtypeStruct((TOK, D), f32), in_sp...  72.4 us
    convert_element_type x1, other arithmetic, local_part(): return total.astype(bf16)  1.6 us

profile of v2, /device:TPU:0, one launch (start us, length us, event | category | flops | bytes accessed | tf_op | source)
XLA Modules:
  0.0 74.0 jit_solution(1431802068267697934)
XLA Ops:
  0.0 72.4 %shard_map.73 = f32[16,3584]{1,0:T(8,128)} custom-call(bf16[16,3584]{1,0:T(8,128)(2,1)} %tokens.1, bf16[16,3584]{1,0:T(8,128)(2,1)} %grads.1, s32[8,16]{1,0:T(8,128)} %bitcast.2, bf16[8,16]{1,0:T(8,128)(2,1)} %bitcast.3, bf16[1,3584,1024]{2,1,0:T(8,128)(2,1)} %w_gate.1, bf16[1,3584,1024]{2,1,0:T(8,128)(2,1)} %w_up.1, bf16[1,1024,3584]{2,1,0:T(8,128)(2,1)} %w_down.1), custom_call_target="tpu_custom_call" | custom-call | flops 9395240960 | bytes 22020096 | tf_op jit(solution)/shard_map/pallas_call | solution.py:391
  72.4 1.6 %convert_element_type.3 = bf16[16,3584]{1,0:T(8,128)(2,1)} convert(f32[16,3584]{1,0:T(8,128)} %shard_map.73) | non-fusion elementwise | flops 57344 | bytes 344064 | tf_op jit(solution)/shard_map/convert_element_type | solution.py:402

commit v3 on v2

--- a/solution.py
+++ b/solution.py
@@ -10,7 +10,7 @@
 F = 1024
 TOK = 16
 TILE = 128
-THERE = ((4, 4, 4), (4, 3, 3), (2, 2, 2))
+THERE = ((2, 2, 2), (4, 4, 4), (4, 3, 3))
 BACK = ((4, 4, 4), (4, 3, 3), (2, 2, 2))
 N_STEP = 512
 LAST_STEP = 256
@@ -161,8 +161,27 @@
                         m_sem.at[3 + kind],
                         (second, step, 0),
                     )
+                if step != 2:
+                    send(
+                        x_buf[n].at[:, 0 : 4 * TOK],
+                        x_buf[n].at[:, rows],
+                        send_sem.at[3],
+                        xb_sem.at[step // 2, n],
+                        (second, step, 0),
+                    )
+
+    for row in there:
+        for n, kind, start, width in row:
+            second = (kind + 1) % 3
+            for half, step in ((0, 1), (1, 3)):
+                rows = slice(step * 64, step * 64 + 64)
+                await_bytes(x_buf[n].at[:, rows], xb_sem.at[half, n])
                 send(
-                    x_buf[n].at[:, 0 : 4 * TOK], x_buf[n].at[:, rows], send_sem.at[3], xb_sem.at[n], (second, step, 0)
+                    x_buf[n].at[half, rows],
+                    x_buf[n].at[half, 128:192],
+                    send_sem.at[8],
+                    xb_sem.at[2, n],
+                    (second, step, 0),
                 )
 
     def make_tables(kind):
@@ -205,7 +224,7 @@
 
     def pack(w, n, kind, start, width):
         third = (kind + 2) % 3
-        await_bytes(x_buf[n].at[:, 4 * TOK : 16 * TOK], xb_sem.at[n])
+        await_bytes(x_buf[n].at[:, 8 * TOK : 12 * TOK], xb_sem.at[2, n])
         land = landing(w, n, start, width)
         for half in range(2):
             rows = jnp.dot(p_buf[kind][...], x_buf[n][half], preferred_element_type=jnp.float32).astype(jnp.bfloat16)
@@ -294,7 +313,7 @@
                 (third, (4 - step) % 4, other),
             )
 
-    def combine(n, kind):
+    def combine(n, kind, start, width):
         second = (kind + 1) % 3
         await_bytes(r_buf[n].at[32:256], rc_sem.at[n])
         part = jnp.dot(q_buf[kind][...], r_buf[n][...], preferred_element_type=jnp.float32)
@@ -303,7 +322,7 @@
             rows = pl.ds(step * 64, 64)
             send(u_buf[n].at[rows], ub_buf[n].at[rows], send_sem.at[6], rb_sem.at[n], (second, 4 - step, 0))
 
-    def reduce_second(n, kind):
+    def reduce_second(n, kind, start, width):
         await_bytes(ub_buf[n].at[64:256], rb_sem.at[n])
         part = u_buf[n][0:64].astype(jnp.float32)
         for step in (1, 2, 3):
@@ -318,7 +337,7 @@
                 (kind, 4 - step, 0),
             )
 
-    def finish(n, start, width):
+    def finish(n, kind, start, width):
         await_bytes(va_buf[n].at[TOK : 4 * TOK], ra_sem.at[n])
         part = v_buf[n][0:TOK].astype(jnp.float32)
         for step in (1, 2, 3):
@@ -326,19 +345,13 @@
         out[:, start : start + width] = part
 
     waves = len(back)
-    for w in range(waves + 3):
-        if w < waves:
-            for n, kind, start, width in back[w]:
-                give(n, kind, start, width)
-        if 1 <= w <= waves:
-            for n, kind, start, width in back[w - 1]:
-                combine(n, kind)
-        if 2 <= w <= waves + 1:
-            for n, kind, start, width in back[w - 2]:
-                reduce_second(n, kind)
-        if w >= 3:
-            for n, kind, start, width in back[w - 3]:
-                finish(n, start, width)
+    order = [(give, w) for w in range(waves)]
+    for w in range(waves + 2):
+        order += [(combine, w), (reduce_second, w - 1), (finish, w - 2)]
+    for stage, w in order:
+        if 0 <= w < waves:
+            for chunk in back[w]:
+                stage(*chunk)
 
     for row in there:
         for n, kind, start, width in row:
@@ -346,7 +359,8 @@
                 await_bytes(m_buf[kind].at[0 : 3 * TOK], send_sem.at[0])
                 await_bytes(m_buf[kind].at[0 : 12 * TOK], send_sem.at[2])
             await_bytes(x_buf[n].at[:, 0 : 3 * TOK], send_sem.at[1])
-            await_bytes(x_buf[n].at[:, 0 : 12 * TOK], send_sem.at[3])
+            await_bytes(x_buf[n].at[:, 0 : 8 * TOK], send_sem.at[3])
+            await_bytes(x_buf[n].at[:, 0 : 4 * TOK], send_sem.at[8])
             await_bytes(s_buf[n].at[:, 32:256], send_sem.at[4])
     for row in back:
         for n, kind, start, width in row:
@@ -378,10 +392,10 @@
         + [
             pltpu.SemaphoreType.DMA((5,)),
             pltpu.SemaphoreType.DMA((2, len(there))),
-            pltpu.SemaphoreType.DMA((8,)),
+            pltpu.SemaphoreType.DMA((10,)),
             pltpu.SemaphoreType.DMA((6,)),
             pltpu.SemaphoreType.DMA((len(there),)),
-            pltpu.SemaphoreType.DMA((len(there),)),
+            pltpu.SemaphoreType.DMA((3, len(there))),
             pltpu.SemaphoreType.DMA((len(there),)),
             pltpu.SemaphoreType.DMA((len(back),)),
             pltpu.SemaphoreType.DMA((len(back),)),

time: 74.2 us -> 71.8 us (0.968)
  Pallas kernels: 72.4 us -> 70 us
    pallas_call x1, Pallas kernels: 72.4 us -> 70 us  [local_part(): pl.pallas_call(body, out_shape=jax.ShapeDtypeStruct((TOK, D), f32), in_sp...]
where the time goes in v3:
time: 71.8 us; the launch traced here: 71.6 us
  Pallas kernels  70 us (97%)
  other arithmetic  1.6 us (2%)
    pallas_call x1, Pallas kernels, local_part(): pl.pallas_call(body, out_shape=jax.ShapeDtypeStruct((TOK, D), f32), in_sp...  70 us
    convert_element_type x1, other arithmetic, local_part(): return total.astype(bf16)  1.6 us

profile of v3, /device:TPU:0, one launch (start us, length us, event | category | flops | bytes accessed | tf_op | source)
XLA Modules:
  0.0 71.6 jit_solution(17282051283514539232)
XLA Ops:
  0.0 70.0 %shard_map.73 = f32[16,3584]{1,0:T(8,128)} custom-call(bf16[16,3584]{1,0:T(8,128)(2,1)} %tokens.1, bf16[16,3584]{1,0:T(8,128)(2,1)} %grads.1, s32[8,16]{1,0:T(8,128)} %bitcast.2, bf16[8,16]{1,0:T(8,128)(2,1)} %bitcast.3, bf16[1,3584,1024]{2,1,0:T(8,128)(2,1)} %w_gate.1, bf16[1,3584,1024]{2,1,0:T(8,128)(2,1)} %w_up.1, bf16[1,1024,3584]{2,1,0:T(8,128)(2,1)} %w_down.1), custom_call_target="tpu_custom_call" | custom-call | flops 9395240960 | bytes 22020096 | tf_op jit(solution)/shard_map/pallas_call | solution.py:405
  70.0 1.6 %convert_element_type.3 = bf16[16,3584]{1,0:T(8,128)(2,1)} convert(f32[16,3584]{1,0:T(8,128)} %shard_map.73) | non-fusion elementwise | flops 57344 | bytes 344064 | tf_op jit(solution)/shard_map/convert_element_type | solution.py:416

commit v4 on v3

--- a/solution.py
+++ b/solution.py
@@ -10,10 +10,10 @@
 F = 1024
 TOK = 16
 TILE = 128
-THERE = ((2, 2, 2), (4, 4, 4), (4, 3, 3))
+THERE = ((4, 4, 4), (4, 3, 3), (2, 2, 2))
 BACK = ((4, 4, 4), (4, 3, 3), (2, 2, 2))
-N_STEP = 512
-LAST_STEP = 256
+N_STEP = 1024
+LAST_STEP = 512
 NT = (((1,), (1,)), ((), ()))
 
 
@@ -346,8 +346,8 @@
 
     waves = len(back)
     order = [(give, w) for w in range(waves)]
-    for w in range(waves + 2):
-        order += [(combine, w), (reduce_second, w - 1), (finish, w - 2)]
+    for stage in (combine, reduce_second, finish):
+        order += [(stage, w) for w in range(waves)]
     for stage, w in order:
         if 0 <= w < waves:
             for chunk in back[w]:

time: 71.8 us -> 70.6 us (0.983)
  Pallas kernels: 70 us -> 68.8 us
    pallas_call x1, Pallas kernels: 70 us -> 68.8 us  [local_part(): pl.pallas_call(body, out_shape=jax.ShapeDtypeStruct((TOK, D), f32), in_sp...]
where the time goes in v4:
time: 70.6 us; the launch traced here: 70.4 us
  Pallas kernels  68.8 us (97%)
  other arithmetic  1.6 us (2%)
    pallas_call x1, Pallas kernels, local_part(): pl.pallas_call(body, out_shape=jax.ShapeDtypeStruct((TOK, D), f32), in_sp...  68.8 us
    convert_element_type x1, other arithmetic, local_part(): return total.astype(bf16)  1.6 us

profile of v4, /device:TPU:0, one launch (start us, length us, event | category | flops | bytes accessed | tf_op | source)
XLA Modules:
  0.0 70.4 jit_solution(8295145258091617453)
XLA Ops:
  0.0 68.8 %shard_map.73 = f32[16,3584]{1,0:T(8,128)} custom-call(bf16[16,3584]{1,0:T(8,128)(2,1)} %tokens.1, bf16[16,3584]{1,0:T(8,128)(2,1)} %grads.1, s32[8,16]{1,0:T(8,128)} %bitcast.2, bf16[8,16]{1,0:T(8,128)(2,1)} %bitcast.3, bf16[1,3584,1024]{2,1,0:T(8,128)(2,1)} %w_gate.1, bf16[1,3584,1024]{2,1,0:T(8,128)(2,1)} %w_up.1, bf16[1,1024,3584]{2,1,0:T(8,128)(2,1)} %w_down.1), custom_call_target="tpu_custom_call" | custom-call | flops 9395240960 | bytes 22020096 | tf_op jit(solution)/shard_map/pallas_call | solution.py:405
  68.8 1.6 %convert_element_type.3 = bf16[16,3584]{1,0:T(8,128)(2,1)} convert(f32[16,3584]{1,0:T(8,128)} %shard_map.73) | non-fusion elementwise | flops 57344 | bytes 344064 | tf_op jit(solution)/shard_map/convert_element_type | solution.py:416
